TPU v7x, 512 devices: a whole 4x8x8 slice. The times are simulated.
512 devices in a mesh: dp: 64 (over z, x, core), mp: 8 (over y).
Axes of the slice: x: 4, y: 8, z: 8, core: 2. Of those that a mesh axis runs over, the one named last changes fastest.
Arguments:
- teacher_in: bfloat16 [64, 1024, 1408], P('dp', 'mp'), may hold values from -8 to 8
- teacher_gain: float32 [1408], replicated, may hold values from 0.5 to 1.5
- teacher_qkv: bfloat16 [3, 1408, 1408], P(None, 'mp'), may hold values from -1 to 1
- teacher_out: bfloat16 [1408, 1408], P('mp'), may hold values from -0.15625 to 0.15625
- student_in: bfloat16 [64, 1024, 1024], P('dp', None, 'mp'), may hold values from -6 to 6
- student_gain: float32 [1024], replicated, may hold values from 0.25 to 1.75
- widen_weight: bfloat16 [1024, 4096], P(None, 'mp'), may hold values from -0.1875 to 0.1875
- narrow_weight: bfloat16 [4096, 1024], P('mp'), may hold values from -0.09375 to 0.09375
- target_head: bfloat16 [1408, 1024], P('mp'), may hold values from -0.1875 to 0.1875
- positions: int32 [64, 512], P('dp'), may hold values from 0 to 1023, as said below
- counts: int32 [64], P('dp'), may hold values from 1 to 512, 16384 in all
Outputs:
- grad_widen: float32 [1024, 4096], P('dp', 'mp')
- grad_narrow: float32 [1024, 4096], P('dp', 'mp')
- losses: float32 [64], P('dp')
Inputs may be any that keep to these rules, and one draw needn't show every extreme that they name: `positions`: the entries of one image's list are distinct; only the first counts of them are live. The counts of all images sum to 16384.
All inputs are finite; a program needn't handle non-finite values. No bound on the sum of `counts` on one device may be relied on, other than what follows from the above.
Results may differ from a plain program's by a relative error of at most 0.02.
Values may be sent and summed in bfloat16 or wider, within the bound.
No kernel may reach another device: no remote copies, remote signals or barrier semaphores. Data moves between devices by JAX's collectives and lax.ppermute only.
A program may use at most 64 MiB of HBM per device.

v0:
```python
import jax
import jax.numpy as jnp
from jax import lax
from jax.sharding import PartitionSpec as P

TD = 1408
TH = 16
EPSILON = 1e-06


def in_order(tiles, dim):
    tiles = jnp.moveaxis(tiles, 0, dim)
    dims = tiles.shape
    return tiles.reshape(*dims[:dim], dims[dim] * dims[dim + 1], *dims[dim + 2 :])


def sent_to_all(array, axis):
    copies = jnp.broadcast_to(array, (lax.axis_size(axis), *array.shape))
    return lax.all_to_all(copies, axis, split_axis=0, concat_axis=0, tiled=True)


def gather_directly(array, axis, dim):
    return in_order(sent_to_all(array, axis), dim)


def rows_for(lines, peers):
    spare = -lines.shape[0] % peers
    if not spare:
        return lines
    return jnp.concatenate([lines, jnp.zeros((spare, *lines.shape[1:]), lines.dtype)])


def total_of(array, axis):
    lines = array.reshape(-1, *array.shape[1:][-1:])
    own = lax.psum_scatter(
        rows_for(lines, lax.axis_size(axis)), axis, scatter_dimension=0, tiled=True
    )
    whole = lax.all_gather(own, axis).reshape(-1, *lines.shape[1:])
    return lax.slice_in_dim(whole, 0, len(lines)).reshape(array.shape)


def of_everyone(array, axis):
    everything = sent_to_all(array, axis)
    return jnp.sum(everything, axis=0)


def packed_total(arrays, axis):
    ends = [0]
    for a in arrays:
        ends.append(ends[-1] + a.size)
    so_far = of_everyone(jnp.concatenate([a.ravel() for a in arrays]), axis)
    return tuple((so_far[b:e].reshape(a.shape) for a, b, e in zip(arrays, ends, ends[1:])))


def cut_along(array, dim, peers):
    dims = array.shape
    tiles = array.reshape(*dims[:dim], peers, dims[dim] // peers, *dims[dim + 1 :])
    return jnp.moveaxis(tiles, dim, 0)


def summed_on_arrival(array, axis, dim):
    peers = lax.axis_size(axis)
    tiles = lax.all_to_all(cut_along(array, dim, peers), axis, 0, 0, tiled=True)
    return jnp.sum(tiles, axis=0)


def layer_norm(values, gain):
    mean_val = jnp.mean(values, axis=-1, keepdims=True)
    centred = values - mean_val
    spread = jnp.mean(centred * centred, axis=-1, keepdims=True)
    return centred * lax.rsqrt(spread + EPSILON) * gain


def gelu_value(pre):
    return 0.5 * pre * (1.0 + lax.erf(pre * 0.7071067811865476))


def gelu_slope(pre):
    return 0.5 * (1.0 + lax.erf(pre * 0.7071067811865476)) + pre * 0.3989422804014327 * jnp.exp(
        -0.5 * pre * pre
    )


def on_device(
    teacher_in,
    teacher_gain,
    teacher_qkv,
    teacher_out,
    student_in,
    student_gain,
    widen_weight,
    narrow_weight,
    target_head,
    positions,
    counts,
):
    patches_local = teacher_in[0]
    slot_total = positions.shape[1]
    picked = positions[0]
    live_count = counts[0]
    head_size = TD // TH
    factor = head_size ** (-0.5)
    local_width = teacher_qkv.shape[1]
    local_heads = local_width // head_size
    gathered = lax.all_gather(patches_local, "mp", axis=0, tiled=True)
    teach_normed = layer_norm(gathered.astype(jnp.float32), teacher_gain).astype(jnp.bfloat16)
    key_rows = jnp.einsum(
        "pi,oi->po", teach_normed, teacher_qkv[1], preferred_element_type=jnp.float32
    ).astype(jnp.bfloat16)
    value_rows = jnp.einsum(
        "pi,oi->po", teach_normed, teacher_qkv[2], preferred_element_type=jnp.float32
    ).astype(jnp.bfloat16)
    query_rows = jnp.einsum(
        "pi,oi->po", teach_normed[picked], teacher_qkv[0], preferred_element_type=jnp.float32
    ).astype(jnp.bfloat16)
    query_heads = query_rows.reshape(slot_total, local_heads, head_size)
    key_heads = key_rows.reshape(-1, local_heads, head_size)
    value_heads = value_rows.reshape(-1, local_heads, head_size)
    scores = (
        jnp.einsum("shd,phd->hsp", query_heads, key_heads, preferred_element_type=jnp.float32)
        * factor
    )
    largest = jnp.max(scores, axis=-1, keepdims=True)
    soft_num = jnp.exp(scores - largest)
    soft_weights = (soft_num / jnp.sum(soft_num, axis=-1, keepdims=True)).astype(jnp.bfloat16)
    attended = jnp.einsum(
        "hsp,phd->shd", soft_weights, value_heads, preferred_element_type=jnp.float32
    )
    attended = attended.astype(jnp.bfloat16).reshape(slot_total, local_width)
    blended = jnp.einsum(
        "sw,ow->so",
        gather_directly(attended, "mp", 1),
        teacher_out,
        preferred_element_type=jnp.float32,
    )
    own_start = lax.axis_index("mp") * local_width
    residual_part = lax.dynamic_slice_in_dim(gathered[picked], own_start, local_width, 1)
    targets = (residual_part.astype(jnp.float32) + blended).astype(jnp.bfloat16)
    slot_ids = jnp.arange(slot_total, dtype=jnp.int32)
    row_weight = jnp.where(
        slot_ids < live_count, 1.0 / live_count.astype(jnp.float32), jnp.zeros((), jnp.float32)
    )
    student_rows = student_in[0][picked]
    student_full = gather_directly(student_rows, "mp", 1)
    student_f32 = student_full.astype(jnp.float32)
    normed_rows = layer_norm(student_f32, student_gain).astype(jnp.bfloat16)
    pre_act = jnp.dot(normed_rows, widen_weight, preferred_element_type=jnp.float32)
    activity = gelu_value(pre_act).astype(jnp.bfloat16)
    branch_sum = total_of(
        jnp.dot(activity, narrow_weight, preferred_element_type=jnp.float32).astype(jnp.bfloat16),
        "mp",
    ).astype(jnp.float32)
    outputs = (student_f32 + branch_sum).astype(jnp.bfloat16)
    predicted = jnp.einsum("rd,cd->rc", outputs, target_head, preferred_element_type=jnp.float32)
    targets32 = targets.astype(jnp.float32)
    inner_sum, pred_sq, target_sq = packed_total(
        (
            jnp.sum(predicted * targets32, axis=-1),
            jnp.sum(predicted * predicted, axis=-1),
            jnp.sum(targets32 * targets32, axis=-1),
        ),
        "mp",
    )
    inv_pred = lax.rsqrt(pred_sq + EPSILON)
    inv_target = lax.rsqrt(target_sq + EPSILON)
    cosine = inner_sum * inv_pred * inv_target
    row_loss = row_weight * (1.0 - cosine)
    pred_slope = (row_weight * cosine * inv_pred * inv_pred)[:, None] * predicted - (
        row_weight * inv_pred * inv_target
    )[:, None] * targets32
    pred_slope = pred_slope.astype(jnp.bfloat16)
    back_sum = lax.psum(
        jnp.einsum("rc,cd->rd", pred_slope, target_head, preferred_element_type=jnp.float32).astype(
            jnp.bfloat16
        ),
        "mp",
    )
    back_act = jnp.einsum("rd,hd->rh", back_sum, narrow_weight, preferred_element_type=jnp.float32)
    back_pre = (back_act * gelu_slope(pre_act)).astype(jnp.bfloat16)
    column_part = normed_rows
    grad_widen = summed_on_arrival(
        jnp.einsum("rd,rh->dh", column_part, back_pre, preferred_element_type=jnp.float32), "dp", 0
    )
    column_part = back_sum
    grad_narrow = summed_on_arrival(
        jnp.einsum("rd,rh->dh", column_part, activity, preferred_element_type=jnp.float32), "dp", 0
    )
    image_loss = jnp.sum(row_loss)
    return (grad_widen, grad_narrow, jnp.reshape(image_loss, (1,)))


def solution(mesh):
    placed = (
        P("dp", "mp", None),
        P(),
        P(None, "mp", None),
        P("mp", None),
        P("dp", None, "mp"),
        P(),
        P(None, "mp"),
        P("mp", None),
        P("mp", None),
        P("dp", None),
        P("dp"),
    )
    return jax.shard_map(
        on_device,
        mesh=mesh,
        in_specs=placed,
        out_specs=(P("dp", "mp"), P("dp", "mp"), P("dp")),
        check_vma=False,
    )
```

profile of v0, /device:TPU:2, one launch (start us, length us, event | category | flops | bytes accessed | tf_op | source)
XLA Modules:
  0.0 403.2 jit_solution(8823197058762961276)
XLA Ops:
  7.2 0.0 copy-start
  7.2 0.0 all-gather.7.cloned.1.call-start
  7.2 0.7 all-gather.7.cloned.1.call-update
  7.9 0.0 reduce-scatter.4.cloned.1.call-start
  8.0 0.7 compare_select_fusion
  8.7 2.0 gather_fusion
  10.7 0.1 copy.33
  10.8 0.1 broadcast_in_dim.14
  10.9 0.0 copy-start.11
  10.9 42.5 %all_to_all.26 = bf16[8,512,128]{1,2,0:T(8,128)(2,1)S(1)} all-to-all(bf16[8,512,128]{1,2,0:T(8,128)(2,1)S(1)} %broadcast_in_dim.14), channel_id=1, replica_groups=mesh['dp'=64,'mp'=8] {'mp'}, dimensions={0} | all-to-all | bytes 2097152 | tf_op jit(solution)/shard_map/all_to_all | solution.py:19
  53.4 0.2 convert_reduce_fusion.1
  53.6 0.3 fusion.10
  54.0 0.3 fusion.13
  54.3 0.3 copy-done.13
  54.6 1.7 multiply_convert_fusion
  56.4 0.0 copy-done.7
  56.4 0.8 copy-done.9
  57.2 1.7 convolution_convert_fusion.1
  58.9 0.0 reduce-scatter.4.cloned.1.call-update
  58.9 13.3 %all-gather.7.cloned.1.call-done = bf16[1,1024,1408]{2,1,0:T(8,128)(2,1)} async-done(((bf16[1,128,1408]{2,1,0:T(8,128)(2,1)}), bf16[1,1024,1408]{2,1,0:T(8,128)(2,1)}) %all-gather.7.cloned.1.call-update) | async-done | bytes 2883600 | tf_op jit(solution)/shard_map/all_gather | solution.py:105
  72.1 2.4 convert_reduce_fusion
  74.5 0.0 copy-start.10
  74.6 0.2 copy-done.1
  74.8 0.9 fusion.3
  75.7 2.5 fusion.5
  78.2 5.5 %gather_fusion.2 = bf16[512,1408]{1,0:T(8,128)(2,1)S(1)} fusion(bf16[1024,1408]{1,0:T(8,128)(2,1)} %fusion.5, s32[1024]{0:T(1024)S(1)} %pad_clamp_fusion), kind=kCustom, calls=%fused_computation.2 | custom fusion | bytes 2885632 | tf_op jit(solution)/shard_map/gather | solution.py:114
  83.8 0.0 copy-start.12
  83.8 2.4 convolution_convert_fusion.4
  86.2 3.1 convolution_convert_fusion.2
  89.3 1.1 convolution_convert_fusion.3
  90.4 3.4 fusion.52
  93.8 3.0 fusion.21
  96.8 1.2 broadcast_in_dim.17
  98.1 4.2 %all-to-all-start.1 = ((bf16[8,512,176]{1,2,0:T(8,128)(2,1)}), bf16[8,512,176]{1,2,0:T(8,128)(2,1)S(1)}, u32[]{:S(2)}, u32[]{:S(2)}) async-start(bf16[8,512,176]{1,2,0:T(8,128)(2,1)} %broadcast_in_dim.17), calls=%async_computation.1 | async-start | bytes 2883584 | tf_op jit(solution)/shard_map/all_to_all | solution.py:19
  102.3 0.2 all-gather.5.cloned.1.call-start
  102.5 22.0 %reduce-scatter.4.cloned.1.call-done = bf16[64,1024]{1,0:T(8,128)(2,1)} async-done(((bf16[512,1024]{1,0:T(8,128)(2,1)}), bf16[64,1024]{1,0:T(8,128)(2,1)}) %reduce-scatter.4.cloned.1.call-update) | async-done | bytes 131088 | tf_op jit(solution)/shard_map/reduce_scatter | solution.py:35
  124.5 0.0 all-gather.5.cloned.1.call-update
  124.6 6.3 %gather_fusion.1 = bf16[512,1408]{1,0:T(8,128)(2,1)} fusion(bf16[1024,1408]{1,0:T(8,128)(2,1)} %bitcast.75, s32[1024]{0:T(1024)S(1)} %pad_clamp_fusion), kind=kCustom, calls=%fused_computation.1 | custom fusion | bytes 2885632 | tf_op jit(solution)/shard_map/gather | solution.py:137
  130.9 1.9 constant_dynamic-slice_fusion
  132.7 1.7 copy.42
  134.5 35.3 %all-gather.5.cloned.1.call-done = bf16[512,1024]{1,0:T(8,128)(2,1)} async-done(((bf16[64,1024]{1,0:T(8,128)(2,1)}), bf16[512,1024]{1,0:T(8,128)(2,1)}) %all-gather.5.cloned.1.call-update) | async-done | bytes 1048592 | tf_op jit(solution)/shard_map/all_gather | solution.py:38
  169.7 2.3 copy.36
  172.0 2.5 fusion.14
  174.5 0.0 all-to-all-done.1
  174.5 1.6 fusion.20
  176.2 0.0 copy-start.6
  176.2 0.4 multiply_reduce_fusion.3
  176.6 0.3 copy-done.4
  176.9 0.6 broadcast_in_dim.18
  177.6 4.3 %all-to-all-start.2 = ((f32[8,1,1536]{2,1,0:T(1,128)}), f32[8,1,1536]{2,1,0:T(1,128)S(1)}, u32[]{:S(2)}, u32[]{:S(2)}) async-start(f32[8,1,1536]{2,1,0:T(1,128)} %broadcast_in_dim.18), calls=%async_computation.2 | async-start | bytes 98304 | tf_op jit(solution)/shard_map/all_to_all | solution.py:19
  181.9 0.0 all-reduce.2.cloned.1.call-start
  182.6 7.5 %all-to-all-done.2 = f32[8,1,1536]{2,1,0:T(1,128)S(1)} async-done(((f32[8,1,1536]{2,1,0:T(1,128)}), f32[8,1,1536]{2,1,0:T(1,128)S(1)}, u32[]{:S(2)}, u32[]{:S(2)}) %all-to-all-start.2) | async-done | bytes 49184 | tf_op jit(solution)/shard_map/all_to_all | solution.py:19
  190.1 0.6 fusion.43
  190.8 2.5 convolution_convert_fusion
  193.3 0.0 all-reduce.2.cloned.1.call-update
  193.3 77.6 %all-reduce.2.cloned.1.call-done = bf16[512,1024]{1,0:T(8,128)(2,1)} async-done(((bf16[512,1024]{1,0:T(8,128)(2,1)}), bf16[512,1024]{1,0:T(8,128)(2,1)}) %all-reduce.2.cloned.1.call-update) | async-done | bytes 1048592 | tf_op jit(solution)/shard_map/psum | solution.py:172
  270.9 4.4 %fusion.22 = f32[64,16,512]{2,1,0:T(8,128)} fusion(bf16[64,16,512]{2,1,0:T(8,128)(2,1)S(1)} %bitcast.78, bf16[512,1024]{1,0:T(8,128)(2,1)} %all-reduce.2.cloned.1.call-done, bf16[512,1024]{1,0:T(8,128)(2,1)S(1)} %copy-done, f32[512,512]{1,0:T(8,128)} %get-tuple-element.13), kind=kOutput, calls=%fused_computation.40 | convolution fusion | flops 1076363264 | bytes 6291456 | tf_op jit(solution)/shard_map/rd,rh->dh/dot_general | solution.py:182
  275.3 10.9 %all-to-all-start.3 = ((f32[64,16,512]{2,1,0:T(8,128)}), f32[64,16,512]{2,1,0:T(8,128)S(1)}, u32[]{:S(2)}, u32[]{:S(2)}) async-start(f32[64,16,512]{2,1,0:T(8,128)} %fusion.22), calls=%async_computation.3 | async-start | bytes 4194304 | tf_op jit(solution)/shard_map/all_to_all | solution.py:63
  286.3 3.4 fusion.53
  289.7 47.9 %all-to-all-done.3 = f32[64,16,512]{2,1,0:T(8,128)S(1)} async-done(((f32[64,16,512]{2,1,0:T(8,128)}), f32[64,16,512]{2,1,0:T(8,128)S(1)}, u32[]{:S(2)}, u32[]{:S(2)}) %all-to-all-start.3) | async-done | bytes 2097184 | tf_op jit(solution)/shard_map/all_to_all | solution.py:63
  337.5 5.6 %all-to-all-start.4 = ((f32[64,16,512]{2,1,0:T(8,128)}), f32[64,16,512]{2,1,0:T(8,128)}, u32[]{:S(2)}, u32[]{:S(2)}) async-start(f32[64,16,512]{2,1,0:T(8,128)} %bitcast.21), calls=%async_computation.4 | async-start | bytes 4194304 | tf_op jit(solution)/shard_map/all_to_all | solution.py:63
  343.2 0.8 reduce_sum.117
  343.9 50.4 %all-to-all-done.4 = f32[64,16,512]{2,1,0:T(8,128)} async-done(((f32[64,16,512]{2,1,0:T(8,128)}), f32[64,16,512]{2,1,0:T(8,128)}, u32[]{:S(2)}, u32[]{:S(2)}) %all-to-all-start.4) | async-done | bytes 2097184 | tf_op jit(solution)/shard_map/all_to_all | solution.py:63
  394.3 2.3 reduce_sum.118
  (28 shorter events, 0.1 us)
Async XLA Ops:
  7.2 50.0 %copy-start = (bf16[512,1024]{1,0:T(8,128)(2,1)S(1)}, bf16[512,1024]{1,0:T(8,128)(2,1)}, u32[]{:S(2)}) copy-start(bf16[512,1024]{1,0:T(8,128)(2,1)} %param.18) | copy-start | bytes 3145732
  7.2 65.0 %all-gather.7.cloned.1.call-start = ((), (), s32[]{:S(2)}) async-start(), calls=%async_computation.8 | async-start | bytes 3244032 | tf_op jit(solution)/shard_map/all_gather | solution.py:105
  7.9 116.6 %reduce-scatter.4.cloned.1.call-start = ((), (), s32[]{:S(2)}) async-start(), calls=%async_computation.9 | async-start | bytes 1179648 | tf_op jit(solution)/shard_map/reduce_scatter | solution.py:35
  10.9 43.1 %copy-start.11 = (f32[1024]{0:T(1024)S(1)}, f32[1024]{0:T(1024)}, u32[]{:S(2)}) copy-start(f32[1024]{0:T(1024)} %param.16) | copy-start | bytes 12292
  53.4 1.2 copy-start.13
  54.6 1.7 copy-start.7
  56.4 0.8 copy-start.9
  72.1 2.7 copy-start.1
  74.5 1.2 copy-start.10
  83.8 2.5 copy-start.12
  86.2 3.1 copy-start.2
  89.3 1.1 copy-start.14
  98.1 76.4 %all-to-all-start.1 = ((bf16[8,512,176]{1,2,0:T(8,128)(2,1)}), bf16[8,512,176]{1,2,0:T(8,128)(2,1)S(1)}, u32[]{:S(2)}, u32[]{:S(2)}) async-start(bf16[8,512,176]{1,2,0:T(8,128)(2,1)} %broadcast_in_dim.17), calls=%async_computation.1 | async-start | bytes 2883584 | tf_op jit(solution)/shard_map/all_to_all | solution.py:19
  102.3 67.4 %all-gather.5.cloned.1.call-start = ((), (), s32[]{:S(2)}) async-start(), calls=%async_computation.7 | async-start | bytes 1179648 | tf_op jit(solution)/shard_map/all_gather | solution.py:38
  174.5 1.6 copy-start.3
  174.5 1.6 copy-start.5
  176.2 0.8 copy-start.4
  176.2 14.6 %copy-start.6 = (bf16[176,1024]{1,0:T(8,128)(2,1)S(1)}, bf16[176,1024]{1,0:T(8,128)(2,1)}, u32[]{:S(2)}) copy-start(bf16[176,1024]{1,0:T(8,128)(2,1)} %param.19) | copy-start | bytes 1081348
  176.9 94.0 %copy-start.8 = (bf16[512,1024]{0,1:T(8,128)(2,1)S(1)}, bf16[512,1024]{0,1:T(8,128)(2,1)}, u32[]{:S(2)}) copy-start(bf16[512,1024]{0,1:T(8,128)(2,1)} %copy-done.7) | copy-start | bytes 3145732
  177.6 12.5 %all-to-all-start.2 = ((f32[8,1,1536]{2,1,0:T(1,128)}), f32[8,1,1536]{2,1,0:T(1,128)S(1)}, u32[]{:S(2)}, u32[]{:S(2)}) async-start(f32[8,1,1536]{2,1,0:T(1,128)} %broadcast_in_dim.18), calls=%async_computation.2 | async-start | bytes 98304 | tf_op jit(solution)/shard_map/all_to_all | solution.py:19
  181.9 89.0 %all-reduce.2.cloned.1.call-start = ((), (), s32[]{:S(2)}) async-start(), calls=%async_computation.6 | async-start | bytes 2097152 | tf_op jit(solution)/shard_map/psum | solution.py:172
  275.3 62.2 %all-to-all-start.3 = ((f32[64,16,512]{2,1,0:T(8,128)}), f32[64,16,512]{2,1,0:T(8,128)S(1)}, u32[]{:S(2)}, u32[]{:S(2)}) async-start(f32[64,16,512]{2,1,0:T(8,128)} %fusion.22), calls=%async_computation.3 | async-start | bytes 4194304 | tf_op jit(solution)/shard_map/all_to_all | solution.py:63
  337.5 56.8 %all-to-all-start.4 = ((f32[64,16,512]{2,1,0:T(8,128)}), f32[64,16,512]{2,1,0:T(8,128)}, u32[]{:S(2)}, u32[]{:S(2)}) async-start(f32[64,16,512]{2,1,0:T(8,128)} %bitcast.21), calls=%async_computation.4 | async-start | bytes 4194304 | tf_op jit(solution)/shard_map/all_to_all | solution.py:63
Sparse Core Ops, SparseCore 0:
  10.1 61.9 all-gather.6
  75.0 49.5 reduce-scatter.3
  126.6 43.0 all-gather.4
  193.4 77.4 all-reduce.1
where the time goes:
time: 404 us; the launch traced here: 403 us
  waiting for transfers between devices  255 us (63%)
  blocking collectives  42.5 us (11%)
  matrix products  28.7 us (7%)
  starting transfers between devices  25.4 us (6%)
  local copies, waits for them, and re-layouts  23.6 us (6%)
  between operations  14.7 us (4%)
  other arithmetic  13.6 us (3%)
    all_to_all x2, waiting for transfers between devices, summed_on_arrival(): tiles = lax.all_to_all(cut_along(array, dim, peers), axis, 0, 0, tiled=True)  98.3 us
    psum x1, waiting for transfers between devices, on_device(): lax.psum(jnp.einsum('rc,cd->rd', pred_slope, target_head, preferred_eleme...  77.6 us
    all_to_all x1, blocking collectives, sent_to_all(): return lax.all_to_all(copies, axis, split_axis=0, concat_axis=0, tiled=True)  42.5 us
    all_gather x1, waiting for transfers between devices, total_of(): whole = lax.all_gather(own, axis).reshape(-1, *lines.shape[1:])  35.3 us
    reduce_scatter x1, waiting for transfers between devices, total_of(): lax.psum_scatter(rows_for(lines, lax.axis_size(axis)), axis, scatter_dime...  22 us
    all_to_all x2, starting transfers between devices, summed_on_arrival(): tiles = lax.all_to_all(cut_along(array, dim, peers), axis, 0, 0, tiled=True)  16.5 us
    all_gather x1, waiting for transfers between devices, on_device(): gathered = lax.all_gather(patches_local, 'mp', axis=0, tiled=True)  13.3 us
    all_to_all x2, starting transfers between devices, sent_to_all(): return lax.all_to_all(copies, axis, split_axis=0, concat_axis=0, tiled=True)  8.57 us
  transfers between devices with their start and end apart: 8, of which 7 were waited for; matrix products, arithmetic and copies ran while one was open for 13% of the time, Pallas kernels for 0%

commit v1 on v0

--- a/solution.py
+++ b/solution.py
@@ -169,11 +169,14 @@
         row_weight * inv_pred * inv_target
     )[:, None] * targets32
     pred_slope = pred_slope.astype(jnp.bfloat16)
-    back_sum = lax.psum(
-        jnp.einsum("rc,cd->rd", pred_slope, target_head, preferred_element_type=jnp.float32).astype(
-            jnp.bfloat16
+    back_sum = jnp.sum(
+        lax.all_gather(
+            jnp.einsum(
+                "rc,cd->rd", pred_slope, target_head, preferred_element_type=jnp.float32
+            ).astype(jnp.bfloat16),
+            "mp",
         ),
-        "mp",
+        axis=0,
     )
     back_act = jnp.einsum("rd,hd->rh", back_sum, narrow_weight, preferred_element_type=jnp.float32)
     back_pre = (back_act * gelu_slope(pre_act)).astype(jnp.bfloat16)

time: 404 us -> 425 us (1.052)
  waiting for transfers between devices: 255 us -> 268 us
  other arithmetic: 13.6 us -> 19.4 us
    all_gather x0 -> x1, waiting for transfers between devices: none -> 93 us  [on_device(): lax.all_gather(jnp.einsum('rc,cd->rd', pred_slope, target_head, preferred...]
    psum x1 -> x0, waiting for transfers between devices: 77.6 us -> none  [on_device(): lax.psum(jnp.einsum('rc,cd->rd', pred_slope, target_head, preferred_eleme...]
    reduce_sum x0 -> x1, other arithmetic: none -> 5.75 us  [on_device(): jnp.sum(lax.all_gather(jnp.einsum('rc,cd->rd', pred_slope, target_head, p...]
where the time goes in v1:
time: 425 us; the launch traced here: 424 us
  waiting for transfers between devices  268 us (63%)
  blocking collectives  42.5 us (10%)
  matrix products  28.8 us (7%)
  local copies, waits for them, and re-layouts  25.9 us (6%)
  starting transfers between devices  25.4 us (6%)
  other arithmetic  19.4 us (5%)
  between operations  14.7 us (3%)
    all_to_all x2, waiting for transfers between devices, summed_on_arrival(): tiles = lax.all_to_all(cut_along(array, dim, peers), axis, 0, 0, tiled=True)  96 us
    all_gather x1, waiting for transfers between devices, on_device(): lax.all_gather(jnp.einsum('rc,cd->rd', pred_slope, target_head, preferred...  93 us
    all_to_all x1, blocking collectives, sent_to_all(): return lax.all_to_all(copies, axis, split_axis=0, concat_axis=0, tiled=True)  42.5 us
    all_gather x1, waiting for transfers between devices, total_of(): whole = lax.all_gather(own, axis).reshape(-1, *lines.shape[1:])  35 us
    reduce_scatter x1, waiting for transfers between devices, total_of(): lax.psum_scatter(rows_for(lines, lax.axis_size(axis)), axis, scatter_dime...  22.3 us
    all_to_all x2, starting transfers between devices, summed_on_arrival(): tiles = lax.all_to_all(cut_along(array, dim, peers), axis, 0, 0, tiled=True)  16.5 us
    all_gather x1, waiting for transfers between devices, on_device(): gathered = lax.all_gather(patches_local, 'mp', axis=0, tiled=True)  13.2 us
    all_to_all x2, starting transfers between devices, sent_to_all(): return lax.all_to_all(copies, axis, split_axis=0, concat_axis=0, tiled=True)  8.57 us
  transfers between devices with their start and end apart: 8, of which 7 were waited for; matrix products, arithmetic and copies ran while one was open for 13% of the time, Pallas kernels for 0%

profile of v1, /device:TPU:2, one launch (start us, length us, event | category | flops | bytes accessed | tf_op | source)
XLA Modules:
  0.0 424.4 jit_solution(818488090292904712)
XLA Ops:
  7.2 0.0 copy-start
  7.2 0.0 all-gather.9.cloned.1.call-start
  7.2 0.7 all-gather.9.cloned.1.call-update
  7.9 0.0 reduce-scatter.4.cloned.1.call-start
  8.0 0.7 compare_select_fusion
  8.7 2.0 gather_fusion
  10.7 0.1 copy.36
  10.8 0.1 broadcast_in_dim.14
  10.9 0.0 copy-start.12
  10.9 42.5 %all_to_all.26 = bf16[8,512,128]{1,2,0:T(8,128)(2,1)S(1)} all-to-all(bf16[8,512,128]{1,2,0:T(8,128)(2,1)S(1)} %broadcast_in_dim.14), channel_id=1, replica_groups=mesh['dp'=64,'mp'=8] {'mp'}, dimensions={0} | all-to-all | bytes 2097152 | tf_op jit(solution)/shard_map/all_to_all | solution.py:19
  53.4 0.2 convert_reduce_fusion.1
  53.6 0.3 fusion.10
  54.0 0.3 fusion.13
  54.3 0.3 copy-done.14
  54.6 1.8 multiply_convert_fusion
  56.5 0.8 copy-done.10
  57.3 1.7 convolution_convert_fusion.1
  58.9 0.0 reduce-scatter.4.cloned.1.call-update
  59.0 13.2 %all-gather.9.cloned.1.call-done = bf16[1,1024,1408]{2,1,0:T(8,128)(2,1)} async-done(((bf16[1,128,1408]{2,1,0:T(8,128)(2,1)}), bf16[1,1024,1408]{2,1,0:T(8,128)(2,1)}) %all-gather.9.cloned.1.call-update) | async-done | bytes 2883600 | tf_op jit(solution)/shard_map/all_gather | solution.py:105
  72.1 2.4 convert_reduce_fusion
  74.5 0.0 copy-start.11
  74.6 0.2 copy-done.1
  74.8 0.9 fusion.3
  75.7 2.5 fusion.5
  78.2 5.5 %gather_fusion.2 = bf16[512,1408]{1,0:T(8,128)(2,1)S(1)} fusion(bf16[1024,1408]{1,0:T(8,128)(2,1)} %fusion.5, s32[1024]{0:T(1024)S(1)} %pad_clamp_fusion), kind=kCustom, calls=%fused_computation.2 | custom fusion | bytes 2885632 | tf_op jit(solution)/shard_map/gather | solution.py:114
  83.8 0.0 copy-start.13
  83.8 2.5 convolution_convert_fusion.4
  86.2 3.1 convolution_convert_fusion.2
  89.3 1.1 convolution_convert_fusion.3
  90.4 3.4 fusion.54
  93.8 3.0 fusion.21
  96.8 1.2 broadcast_in_dim.17
  98.1 4.2 all-to-all-start.1
  102.3 0.2 all-gather.7.cloned.1.call-start
  102.5 22.3 %reduce-scatter.4.cloned.1.call-done = bf16[64,1024]{1,0:T(8,128)(2,1)} async-done(((bf16[512,1024]{1,0:T(8,128)(2,1)}), bf16[64,1024]{1,0:T(8,128)(2,1)}) %reduce-scatter.4.cloned.1.call-update) | async-done | bytes 131088 | tf_op jit(solution)/shard_map/reduce_scatter | solution.py:35
  124.8 0.0 all-gather.7.cloned.1.call-update
  124.8 6.3 %gather_fusion.1 = bf16[512,1408]{1,0:T(8,128)(2,1)} fusion(bf16[1024,1408]{1,0:T(8,128)(2,1)} %bitcast.79, s32[1024]{0:T(1024)S(1)} %pad_clamp_fusion), kind=kCustom, calls=%fused_computation.1 | custom fusion | bytes 2885632 | tf_op jit(solution)/shard_map/gather | solution.py:137
  131.1 1.9 constant_dynamic-slice_fusion
  133.0 1.7 copy.46
  134.7 35.0 %all-gather.7.cloned.1.call-done = bf16[512,1024]{1,0:T(8,128)(2,1)} async-done(((bf16[64,1024]{1,0:T(8,128)(2,1)}), bf16[512,1024]{1,0:T(8,128)(2,1)}) %all-gather.7.cloned.1.call-update) | async-done | bytes 1048592 | tf_op jit(solution)/shard_map/all_gather | solution.py:38
  169.7 2.3 copy.39
  172.0 2.5 fusion.14
  174.5 1.6 fusion.20
  176.2 0.0 copy-start.7
  176.2 0.4 multiply_reduce_fusion.3
  176.6 0.3 copy-done.5
  176.9 0.6 broadcast_in_dim.18
  177.5 4.3 %all-to-all-start.2 = ((f32[8,1,1536]{2,1,0:T(1,128)}), f32[8,1,1536]{2,1,0:T(1,128)S(1)}, u32[]{:S(2)}, u32[]{:S(2)}) async-start(f32[8,1,1536]{2,1,0:T(1,128)} %broadcast_in_dim.18), calls=%async_computation.2 | async-start | bytes 98304 | tf_op jit(solution)/shard_map/all_to_all | solution.py:19
  181.9 0.0 all-gather.11.cloned.1.call-start
  182.6 7.5 %all-to-all-done.2 = f32[8,1,1536]{2,1,0:T(1,128)S(1)} async-done(((f32[8,1,1536]{2,1,0:T(1,128)}), f32[8,1,1536]{2,1,0:T(1,128)S(1)}, u32[]{:S(2)}, u32[]{:S(2)}) %all-to-all-start.2) | async-done | bytes 49184 | tf_op jit(solution)/shard_map/all_to_all | solution.py:19
  190.1 0.6 fusion.45
  190.7 2.4 convolution_convert_fusion
  193.2 0.0 all-gather.11.cloned.1.call-update
  193.2 93.0 %all-gather.11.cloned.1.call-done = bf16[4096,1024]{1,0:T(8,128)(2,1)} async-done(((bf16[512,1024]{1,0:T(8,128)(2,1)}), bf16[4096,1024]{1,0:T(8,128)(2,1)}) %all-gather.11.cloned.1.call-update) | async-done | bytes 8388624 | tf_op jit(solution)/shard_map/all_gather | solution.py:173
  286.2 5.8 %reduce_sum.129 = bf16[512,1024]{1,0:T(8,128)(2,1)S(1)} reduce(bf16[8,512,1024]{2,1,0:T(8,128)(2,1)} %bitcast.80, bf16[]{:T(256)} %constant.15.clone.1), dimensions={0}, to_apply=%region_11.12 | reduce | flops 3670016 | bytes 9437186 | tf_op jit(solution)/shard_map/reduce_sum | solution.py:172
  292.0 4.5 %fusion.22 = f32[64,16,512]{2,1,0:T(8,128)} fusion(bf16[64,16,512]{2,1,0:T(8,128)(2,1)S(1)} %bitcast.85, bf16[512,1024]{1,0:T(8,128)(2,1)S(1)} %reduce_sum.129, bf16[512,1024]{1,0:T(8,128)(2,1)S(1)} %copy-done, f32[512,512]{1,0:T(8,128)} %get-tuple-element.13), kind=kOutput, calls=%fused_computation.40 | convolution fusion | flops 1076363264 | bytes 6291456 | tf_op jit(solution)/shard_map/rd,rh->dh/dot_general | solution.py:185
  296.5 10.9 %all-to-all-start.3 = ((f32[64,16,512]{2,1,0:T(8,128)}), f32[64,16,512]{2,1,0:T(8,128)S(1)}, u32[]{:S(2)}, u32[]{:S(2)}) async-start(f32[64,16,512]{2,1,0:T(8,128)} %fusion.22), calls=%async_computation.3 | async-start | bytes 4194304 | tf_op jit(solution)/shard_map/all_to_all | solution.py:63
  307.4 2.3 copy.42
  309.7 3.4 fusion.29
  313.1 45.6 %all-to-all-done.3 = f32[64,16,512]{2,1,0:T(8,128)S(1)} async-done(((f32[64,16,512]{2,1,0:T(8,128)}), f32[64,16,512]{2,1,0:T(8,128)S(1)}, u32[]{:S(2)}, u32[]{:S(2)}) %all-to-all-start.3) | async-done | bytes 2097184 | tf_op jit(solution)/shard_map/all_to_all | solution.py:63
  358.7 5.6 %all-to-all-start.4 = ((f32[64,16,512]{2,1,0:T(8,128)}), f32[64,16,512]{2,1,0:T(8,128)}, u32[]{:S(2)}, u32[]{:S(2)}) async-start(f32[64,16,512]{2,1,0:T(8,128)} %fusion.29), calls=%async_computation.4 | async-start | bytes 4194304 | tf_op jit(solution)/shard_map/all_to_all | solution.py:63
  364.3 0.8 reduce_sum.130
  365.1 50.4 %all-to-all-done.4 = f32[64,16,512]{2,1,0:T(8,128)} async-done(((f32[64,16,512]{2,1,0:T(8,128)}), f32[64,16,512]{2,1,0:T(8,128)}, u32[]{:S(2)}, u32[]{:S(2)}) %all-to-all-start.4) | async-done | bytes 2097184 | tf_op jit(solution)/shard_map/all_to_all | solution.py:63
  415.5 2.3 reduce_sum.131
  (32 shorter events, 0.1 us)
Async XLA Ops:
  7.2 50.1 %copy-start = (bf16[512,1024]{1,0:T(8,128)(2,1)S(1)}, bf16[512,1024]{1,0:T(8,128)(2,1)}, u32[]{:S(2)}) copy-start(bf16[512,1024]{1,0:T(8,128)(2,1)} %param.18) | copy-start | bytes 3145732
  7.2 65.0 %all-gather.9.cloned.1.call-start = ((), (), s32[]{:S(2)}) async-start(), calls=%async_computation.7 | async-start | bytes 3244032 | tf_op jit(solution)/shard_map/all_gather | solution.py:105
  7.9 116.9 %reduce-scatter.4.cloned.1.call-start = ((), (), s32[]{:S(2)}) async-start(), calls=%async_computation.9 | async-start | bytes 1179648 | tf_op jit(solution)/shard_map/reduce_scatter | solution.py:35
  10.9 43.1 %copy-start.12 = (f32[1024]{0:T(1024)S(1)}, f32[1024]{0:T(1024)}, u32[]{:S(2)}) copy-start(f32[1024]{0:T(1024)} %param.16) | copy-start | bytes 12292
  53.4 1.2 copy-start.14
  54.6 1.8 copy-start.8
  56.5 0.8 copy-start.10
  72.1 2.7 copy-start.1
  74.5 1.2 copy-start.11
  83.8 2.5 copy-start.13
  86.2 3.1 copy-start.2
  89.3 1.1 copy-start.15
  98.1 76.4 %all-to-all-start.1 = ((bf16[8,512,176]{1,2,0:T(8,128)(2,1)}), bf16[8,512,176]{1,2,0:T(8,128)(2,1)S(1)}, u32[]{:S(2)}, u32[]{:S(2)}) async-start(bf16[8,512,176]{1,2,0:T(8,128)(2,1)} %broadcast_in_dim.17), calls=%async_computation.1 | async-start | bytes 2883584 | tf_op jit(solution)/shard_map/all_to_all | solution.py:19
  102.3 67.4 %all-gather.7.cloned.1.call-start = ((), (), s32[]{:S(2)}) async-start(), calls=%async_computation.6 | async-start | bytes 1179648 | tf_op jit(solution)/shard_map/all_gather | solution.py:38
  174.5 1.6 copy-start.3
  174.5 1.6 copy-start.6
  176.2 0.7 copy-start.5
  176.2 14.6 %copy-start.7 = (bf16[176,1024]{1,0:T(8,128)(2,1)S(1)}, bf16[176,1024]{1,0:T(8,128)(2,1)}, u32[]{:S(2)}) copy-start(bf16[176,1024]{1,0:T(8,128)(2,1)} %param.19) | copy-start | bytes 1081348
  177.5 12.5 %all-to-all-start.2 = ((f32[8,1,1536]{2,1,0:T(1,128)}), f32[8,1,1536]{2,1,0:T(1,128)S(1)}, u32[]{:S(2)}, u32[]{:S(2)}) async-start(f32[8,1,1536]{2,1,0:T(1,128)} %broadcast_in_dim.18), calls=%async_computation.2 | async-start | bytes 98304 | tf_op jit(solution)/shard_map/all_to_all | solution.py:19
  181.9 104.4 %all-gather.11.cloned.1.call-start = ((), (), s32[]{:S(2)}) async-start(), calls=%async_computation.8 | async-start | bytes 9437184 | tf_op jit(solution)/shard_map/all_gather | solution.py:173
  286.2 5.8 %copy-start.9 = (bf16[512,1024]{0,1:T(8,128)(2,1)S(1)}, bf16[512,1024]{0,1:T(8,128)(2,1)}, u32[]{:S(2)}) copy-start(bf16[512,1024]{0,1:T(8,128)(2,1)} %copy-done.8) | copy-start | bytes 3145732
  292.0 4.5 %copy-start.4 = (bf16[512,1024]{1,0:T(8,128)(2,1)}, bf16[512,1024]{1,0:T(8,128)(2,1)S(1)}, u32[]{:S(2)}) copy-start(bf16[512,1024]{1,0:T(8,128)(2,1)S(1)} %reduce_sum.129) | copy-start | bytes 3145732
  296.5 62.2 %all-to-all-start.3 = ((f32[64,16,512]{2,1,0:T(8,128)}), f32[64,16,512]{2,1,0:T(8,128)S(1)}, u32[]{:S(2)}, u32[]{:S(2)}) async-start(f32[64,16,512]{2,1,0:T(8,128)} %fusion.22), calls=%async_computation.3 | async-start | bytes 4194304 | tf_op jit(solution)/shard_map/all_to_all | solution.py:63
  358.7 56.8 %all-to-all-start.4 = ((f32[64,16,512]{2,1,0:T(8,128)}), f32[64,16,512]{2,1,0:T(8,128)}, u32[]{:S(2)}, u32[]{:S(2)}) async-start(f32[64,16,512]{2,1,0:T(8,128)} %fusion.29), calls=%async_computation.4 | async-start | bytes 4194304 | tf_op jit(solution)/shard_map/all_to_all | solution.py:63
Sparse Core Ops, SparseCore 0:
  10.1 61.9 all-gather.8
  75.0 49.8 reduce-scatter.3
  126.9 42.7 all-gather.6
  193.3 92.8 all-gather.10
